TPU v7x, 32 devices: a whole 2x2x4 slice. The times are simulated.
32 devices in a mesh: dom: 2 (over x), tx: 2 (over core), cell: 8 (over z, y).
Axes of the slice: x: 2, y: 2, z: 4, core: 2. Of those that a mesh axis runs over, the one named last changes fastest.
Arguments:
- sensitivity: bfloat16 [4096, 16384], P(('dom', 'tx'), 'cell'), parts along dimension 0, may hold values from -0.25 to 0.25
- cell_weight: float32 [32768], P(('dom', 'cell')), parts along dimension 0, may hold values from 0.05 to 1
- pair_mask: int32 [16, 8], P('dom'), parts along dimension 0, may hold values from 0 to 1, as said below
- level_index: int32 [16], P('dom'), parts along dimension 0, may hold values from 0 to 3
- damp_levels: float32 [8], P('dom'), parts along dimension 0, may hold values from 0.5 to 8
Outputs:
- gram: float32 [4096, 2048], P(('dom', 'cell'), 'tx'), parts along dimension 0
There are 2 independent parts, one for each index of `dom`. A program takes and returns all parts, laid end to end along the dimension named above; each array names one. Nothing has to cross between parts.
Inputs may be any that keep to these rules, and one draw needn't show every extreme that they name: `pair_mask`: symmetric, with ones on the diagonal.
All inputs are finite; a program needn't handle non-finite values.
Results may differ from a plain program's by a relative error of at most 0.00085.
Values may be sent and summed in bfloat16 or wider, within the bound.
A program may use at most 64 MiB of HBM per device.

v0:
```python
import jax
import jax.numpy as jnp
from jax import lax
from jax.sharding import PartitionSpec as P


def contract(left, right):
    return lax.dot_general(
        left, right, (((1,), (1,)), ((), ())), preferred_element_type=jnp.float32
    )


def local(sensitivity, cell_weight, pair_mask, level_index, damp_levels):
    own_rows = sensitivity.shape[0]
    weighted = (sensitivity.astype(jnp.float32) * cell_weight[None, :]).astype(jnp.bfloat16)
    everyone = lax.all_gather(sensitivity, "tx", axis=0, tiled=True)
    total_rows = everyone.shape[0]
    part_rows = total_rows // lax.axis_size("cell")
    groups = pair_mask.shape[0]
    group_rows = total_rows // groups
    tx_pos = lax.axis_index("tx")
    cell_pos = lax.axis_index("cell")
    mask_float = pair_mask.astype(jnp.float32)
    summed = lax.psum_scatter(contract(everyone, weighted), "cell", scatter_dimension=0, tiled=True)
    row_ids = cell_pos * part_rows + jnp.arange(part_rows, dtype=jnp.int32)
    col_ids = tx_pos * own_rows + jnp.arange(own_rows, dtype=jnp.int32)
    group_iota = jnp.arange(groups, dtype=jnp.int32)
    row_onehot = (row_ids[:, None] // group_rows == group_iota[None, :]).astype(jnp.float32)
    col_onehot = (col_ids[:, None] // group_rows == group_iota[None, :]).astype(jnp.float32)
    tile_mask = jnp.dot(
        jnp.dot(row_onehot, mask_float, precision=lax.Precision.HIGHEST),
        col_onehot.T,
        precision=lax.Precision.HIGHEST,
    )
    level_onehot = (
        level_index[:, None] == jnp.arange(damp_levels.shape[0], dtype=jnp.int32)[None, :]
    ).astype(jnp.float32)
    group_damp = jnp.sum(level_onehot * damp_levels[None, :], axis=1)
    row_damp = jnp.sum(row_onehot * group_damp[None, :], axis=1)
    diagonal = (row_ids[:, None] == col_ids[None, :]).astype(jnp.float32)
    return summed * tile_mask + diagonal * row_damp[:, None]


def solution(mesh):
    in_specs = (P(("dom", "tx"), "cell"), P(("dom", "cell")), P("dom", None), P("dom"), P("dom"))
    out_specs = P(("dom", "cell"), "tx")
    return jax.shard_map(local, mesh=mesh, in_specs=in_specs, out_specs=out_specs, check_vma=False)
```

profile of v0, /device:TPU:1, one launch (start us, length us, event | category | flops | bytes accessed | tf_op | source)
XLA Modules:
  0.0 206.8 jit_solution(7911738041601467554)
XLA Ops:
  6.5 0.0 all-gather.2.cloned.1.call-start
  6.5 0.7 all-gather.2.cloned.1.call-update
  7.3 0.0 reduce-scatter.2.cloned.1.call-start
  7.3 23.9 %all-gather.2.cloned.1.call-done = bf16[2048,2048]{1,0:T(8,128)(2,1)} async-done(((bf16[1024,2048]{1,0:T(8,128)(2,1)}), bf16[2048,2048]{1,0:T(8,128)(2,1)}) %all-gather.2.cloned.1.call-update) | async-done | bytes 8388624 | tf_op jit(solution)/shard_map/all_gather | solution.py:16
  31.2 14.6 %convolution_bitcast_fusion = f32[2048,1024]{0,1:T(8,128)} fusion(bf16[2048,2048]{1,0:T(8,128)(2,1)} %all-gather.2.cloned.1.call-done, bf16[1024,2048]{1,0:T(8,128)(2,1)} %param.5, f32[2048]{0:T(1024)} %param.6), kind=kOutput, calls=%fused_computation.1 | convolution fusion | flops 8596226048 | bytes 20979712 | tf_op jit(solution)/shard_map/dot_general | solution.py:8
  45.9 0.0 copy-start.1
  45.9 0.0 copy-start.2
  45.9 0.0 copy-start
  45.9 0.0 reduce-scatter.2.cloned.1.call-update
  45.9 0.6 copy-done.1
  46.5 0.0 copy-done.2
  46.5 0.1 select_reduce_fusion.1
  46.6 0.1 select_reduce_fusion
  46.7 0.0 copy-done
  46.7 0.3 fusion.3
  47.0 149.4 %reduce-scatter.2.cloned.1.call-done = f32[256,1024]{0,1:T(8,128)} async-done(((f32[2048,1024]{0,1:T(8,128)}), f32[256,1024]{0,1:T(8,128)}) %reduce-scatter.2.cloned.1.call-update) | async-done | bytes 1048592 | tf_op jit(solution)/shard_map/reduce_scatter | solution.py:24
  196.4 2.3 %fusion.1 = f32[256,1024]{0,1:T(8,128)S(1)} fusion(f32[256,1024]{0,1:T(8,128)} %reduce-scatter.2.cloned.1.call-done, f32[256,8]{1,0:T(8,128)S(1)} %fusion.3, f32[256]{0:T(256)S(1)} %select_reduce_fusion, s32[256]{0:T(256)S(1)} %get-tuple-element.6, s32[1024]{0:T(1024)S(1)} %get-tuple-element.8, s32[1024]{0:T(1024)S(1)} %get-tuple-element.7), kind=kOutput, calls=%fused_computation.4 | convolution fusion | flops 26222592 | bytes 2115584 | tf_op jit(solution)/shard_map/dot_general | solution.py:30
  198.7 1.3 copy.9
  (2 shorter events, 0.0 us)
Async XLA Ops:
  6.5 24.7 %all-gather.2.cloned.1.call-start = ((), (), s32[]{:S(2)}) async-start(), calls=%async_computation.1 | async-start | bytes 12582912 | tf_op jit(solution)/shard_map/all_gather | solution.py:16
  7.3 189.1 %reduce-scatter.2.cloned.1.call-start = ((), (), s32[]{:S(2)}) async-start(), calls=%async_computation.2 | async-start | bytes 9437184 | tf_op jit(solution)/shard_map/reduce_scatter | solution.py:24
  45.9 0.7 copy-start.1
  45.9 0.7 copy-start.2
  45.9 0.8 copy-start
Sparse Core Ops, SparseCore 0:
  8.9 22.3 all-gather.1
  46.0 150.3 reduce-scatter.1
where the time goes:
time: 208 us; the launch traced here: 207 us
  waiting for transfers between devices  174 us (84%)
  matrix products  17.2 us (8%)
  between operations  13.4 us (6%)
    reduce_scatter x1, waiting for transfers between devices, local(): lax.psum_scatter(contract(everyone, weighted), 'cell', scatter_dimension=...  149 us
    all_gather x1, waiting for transfers between devices, local(): everyone = lax.all_gather(sensitivity, 'tx', axis=0, tiled=True)  23.9 us
    dot_general x1, matrix products, contract(): lax.dot_general(left, right, (((1,), (1,)), ((), ())), preferred_element_...  14.6 us
  transfers between devices with their start and end apart: 2, of which 2 were waited for; matrix products, arithmetic and copies ran while one was open for 0% of the time, Pallas kernels for 0%

commit v1 on v0

v1 whole, which is shorter than its diff:
```python
import functools

import jax
import jax.numpy as jnp
from jax import lax
from jax.experimental import pallas as pl
from jax.experimental.pallas import tpu as pltpu
from jax.sharding import PartitionSpec as P

MESH = pl.DeviceIdType.MESH
WIRE = jnp.int16
TOP = 32752.0
HEAD = 16


def contract(left, right):
    return lax.dot_general(
        left, right, (((1,), (1,)), ((), ())), preferred_element_type=jnp.float32
    )


def write(ref, value):
    side = value.shape[0]
    peak = jnp.maximum(jnp.max(jnp.abs(value), axis=0, keepdims=True), 2.0**-60)
    power = jnp.ceil(jnp.log2(peak))
    ref[pl.ds(0, side), :] = jnp.round(value * (jnp.exp2(-power) * TOP)).astype(jnp.int32).astype(WIRE)
    head = jnp.broadcast_to(power.astype(jnp.int32), (HEAD, value.shape[1]))
    ref[pl.ds(side, HEAD), :] = head.astype(WIRE)


def read(ref):
    side = ref.shape[0] - HEAD
    power = ref[pl.ds(side, HEAD), :].astype(jnp.int32).astype(jnp.float32)[:1, :]
    whole = ref[pl.ds(0, side), :].astype(jnp.int32).astype(jnp.float32)
    return whole * (jnp.exp2(power) * (1.0 / TOP))


def gram_kernel(
    side, w_ref, s_ref, out_ref,
    sall, wgt, ysend, yrecv, zsend, zrecv, acc, msend, mrecv,
    load_sem, gsend_sem, grecv_sem, ysend_sem, yrecv_sem, zsend_sem, zrecv_sem, msend_sem, mrecv_sem,
):
    t = lax.axis_index("tx")
    c = lax.axis_index("cell")
    z, y = c // 2, c % 2

    def block(r):
        return pl.ds(pl.multiple_of(r * side, side), side)

    def load(i):
        return pltpu.make_async_copy(
            s_ref.at[pl.ds(i * side, side), :], sall.at[0, pl.ds(i * side, side), :], load_sem.at[i]
        )

    for i in range(4):
        load(i).start()

    barrier = pltpu.get_barrier_semaphore()
    for k in range(1, 16):
        pl.semaphore_signal(
            barrier, inc=1,
            device_id={"tx": (t + k // 8) % 2, "cell": (c + k % 8) % 8},
            device_id_type=MESH,
        )

    def gather(r):
        return pltpu.make_async_remote_copy(
            src_ref=s_ref.at[block(r), :], dst_ref=sall.at[1, block(r), :],
            send_sem=gsend_sem.at[r], recv_sem=grecv_sem.at[r],
            device_id={"tx": 1 - t}, device_id_type=MESH,
        )

    pl.semaphore_wait(barrier, 15)
    for r in ((1 - y) + 2, 1 - y, y + 2, y):
        gather(r).start()

    for i in range(4):
        load(i).wait()
        rows = pl.ds(i * side, side)
        wgt[rows, :] = (sall[0, rows, :].astype(jnp.float32) * w_ref[...]).astype(jnp.bfloat16)

    def place(i, a):
        r = a + 2 * (i % 2)
        e = i // 2
        half = (r + e) // 4
        return r, (r + e) % 4, half, r + e == 4

    def product(i, a):
        r, q, half, first = place(i, a)

        @pl.when(first)
        def _():
            gather(r).wait_recv()

        return contract(sall[half, block(r), :], wgt[block(q), :])

    def ycopy(i):
        return pltpu.make_async_remote_copy(
            src_ref=ysend.at[i], dst_ref=yrecv.at[i],
            send_sem=ysend_sem.at[i], recv_sem=yrecv_sem.at[i],
            device_id={"cell": 2 * z + 1 - y}, device_id_type=MESH,
        )

    def zcopy(i, q, owner, source):
        return pltpu.make_async_remote_copy(
            src_ref=zsend.at[i], dst_ref=zrecv.at[source, q],
            send_sem=zsend_sem.at[i], recv_sem=zrecv_sem.at[source, q],
            device_id={"cell": 2 * owner + y}, device_id_type=MESH,
        )

    def mcopy(q, slot):
        return pltpu.make_async_remote_copy(
            src_ref=msend.at[q], dst_ref=mrecv.at[slot],
            send_sem=msend_sem.at[q], recv_sem=mrecv_sem.at[slot],
            device_id={"cell": 4 * t + q, "tx": c // 4}, device_id_type=MESH,
        )

    def first_phase(i, carry):
        write(ysend.at[i], product(i, 1 - y))
        ycopy(i).start()
        return carry

    lax.fori_loop(0, 10, first_phase, 0)

    def owner_of(i):
        r, q, half, _ = place(i, y)
        return q, 2 * ((t + half) % 2) + r // 2

    def second_phase(i, carry):
        q, owner = owner_of(i)
        part = product(i, y)
        ycopy(i).wait_recv()
        part = part + read(yrecv.at[i])

        @pl.when(owner == z)
        def _():
            acc[q] = part

        @pl.when(owner != z)
        def _():
            write(zsend.at[i], part)
            zcopy(i, q, owner, z).start()

        return carry

    lax.fori_loop(0, 10, second_phase, 0)

    rank = c % 4
    same = c // 4 == t

    def held(q):
        return jnp.where(same, q >= rank, q <= rank)

    for q in range(4):
        columns = pl.ds(q * side, side)

        @pl.when(held(q))
        def _():
            total = acc[q]
            for k in range(1, 4):
                source = (z + k) % 4
                zcopy(0, q, z, source).wait_recv()
                total = total + read(zrecv.at[source, q])
            out_ref[:, columns] = total

            @pl.when(q != rank)
            def _():
                write(msend.at[q], total)
                mcopy(q, rank).start()

    for q in range(4):
        columns = pl.ds(q * side, side)

        @pl.when(jnp.logical_not(held(q)))
        def _():
            mcopy(q, q).wait_recv()
            out_ref[:, columns] = read(mrecv.at[q]).T

    for r in range(4):
        gather(r).wait_send()

    def drain(i, carry):
        ycopy(i).wait_send()
        q, owner = owner_of(i)

        @pl.when(owner != z)
        def _():
            zcopy(i, q, owner, z).wait_send()

        return carry

    lax.fori_loop(0, 10, drain, 0)
    for q in range(4):
        @pl.when(jnp.logical_and(held(q), q != rank))
        def _():
            mcopy(q, rank).wait_send()


def gram_sums(sensitivity, cell_weight, groups):
    own_rows, cells = sensitivity.shape
    side = 2 * own_rows // groups
    tile = (side, side)
    wire = (side + HEAD, side)
    dma = pltpu.SemaphoreType.DMA
    return pl.pallas_call(
        functools.partial(gram_kernel, side),
        out_shape=jax.ShapeDtypeStruct((side, own_rows), jnp.float32),
        in_specs=[
            pl.BlockSpec(memory_space=pltpu.VMEM),
            pl.BlockSpec(memory_space=pl.ANY),
        ],
        out_specs=pl.BlockSpec(memory_space=pltpu.VMEM),
        scratch_shapes=[
            pltpu.VMEM((2, own_rows, cells), jnp.bfloat16),
            pltpu.VMEM((own_rows, cells), jnp.bfloat16),
            pltpu.VMEM((10,) + wire, WIRE),
            pltpu.VMEM((10,) + wire, WIRE),
            pltpu.VMEM((10,) + wire, WIRE),
            pltpu.VMEM((4, 4) + wire, WIRE),
            pltpu.VMEM((4,) + tile, jnp.float32),
            pltpu.VMEM((4,) + wire, WIRE),
            pltpu.VMEM((4,) + wire, WIRE),
            dma((4,)), dma((4,)), dma((4,)),
            dma((10,)), dma((10,)), dma((10,)), dma((4, 4)), dma((4,)), dma((4,)),
        ],
        compiler_params=pltpu.CompilerParams(
            collective_id=0, has_side_effects=True, vmem_limit_bytes=48 * 1024 * 1024
        ),
        cost_estimate=pl.CostEstimate(
            flops=2 * 20 * side * side * cells, bytes_accessed=own_rows * cells * 2, transcendentals=0
        ),
    )(cell_weight[None, :], sensitivity)


def plain_sums(sensitivity, cell_weight):
    weighted = (sensitivity.astype(jnp.float32) * cell_weight[None, :]).astype(jnp.bfloat16)
    everyone = lax.all_gather(sensitivity, "tx", axis=0, tiled=True)
    return lax.psum_scatter(contract(everyone, weighted), "cell", scatter_dimension=0, tiled=True)


def local(sensitivity, cell_weight, pair_mask, level_index, damp_levels):
    own_rows = sensitivity.shape[0]
    groups = pair_mask.shape[0]
    total_rows = own_rows * lax.axis_size("tx")
    part_rows = total_rows // lax.axis_size("cell")
    group_rows = total_rows // groups
    tx_pos = lax.axis_index("tx")
    cell_pos = lax.axis_index("cell")
    if lax.axis_size("tx") == 2 and lax.axis_size("cell") == 8 and groups == 8:
        summed = gram_sums(sensitivity, cell_weight, groups)
    else:
        summed = plain_sums(sensitivity, cell_weight)
    group = cell_pos * part_rows // group_rows
    col_groups = tx_pos * own_rows // group_rows + jnp.arange(own_rows // group_rows, dtype=jnp.int32)
    mask_row = pair_mask[group][col_groups].astype(jnp.float32)
    damp = damp_levels[level_index[group]]
    row_ids = cell_pos * part_rows + lax.broadcasted_iota(jnp.int32, summed.shape, 0)
    col_ids = tx_pos * own_rows + lax.broadcasted_iota(jnp.int32, summed.shape, 1)
    col_mask = jnp.repeat(mask_row, group_rows)[None, :]
    return summed * col_mask + jnp.where(row_ids == col_ids, damp, 0.0)


def solution(mesh):
    in_specs = (P(("dom", "tx"), "cell"), P(("dom", "cell")), P("dom", None), P("dom"), P("dom"))
    out_specs = P(("dom", "cell"), "tx")
    return jax.shard_map(local, mesh=mesh, in_specs=in_specs, out_specs=out_specs, check_vma=False)
```

time: 208 us -> 61.6 us (0.30)
  waiting for transfers between devices: 174 us -> 0 us
  Pallas kernels: 0 us -> 51.4 us
  matrix products: 17.2 us -> 0 us
  between operations: 13.4 us -> 1.98 us
  local copies, waits for them, and re-layouts: 1.91 us -> 6.16 us
    reduce_scatter x1 -> x0, waiting for transfers between devices: 149 us -> none  [local(): lax.psum_scatter(contract(everyone, weighted), 'cell', scatter_dimension=...]
    pallas_call x0 -> x1, Pallas kernels: none -> 51.4 us  [gram_sums(): pl.pallas_call(functools.partial(gram_kernel, side), out_shape=jax.ShapeD...]
    all_gather x1 -> x0, waiting for transfers between devices: 23.9 us -> none  [local(): everyone = lax.all_gather(sensitivity, 'tx', axis=0, tiled=True)]
    dot_general x3 -> x0, matrix products: 17.2 us -> none  [the longest x1 14.6 us: contract(): lax.dot_general(left, right, (((1,), (1,)), ((), ())), preferred_element_...]
    dynamic_slice x0 -> x2, local copies, waits for them, and re-layouts: none -> 2.55 us  [local(): damp = damp_levels[level_index[group]]]
    unnamed x6 -> x8, local copies, waits for them, and re-layouts: 0.6 us -> 2.97 us
  transfers between devices with their start and end apart: 2 -> 0, of which waited for: 2 -> 0; matrix products, arithmetic and copies ran while one was open for 0% -> 0% of each run, Pallas kernels for 0% -> 0%
where the time goes in v1:
time: 61.6 us; the launch traced here: 61.3 us
  Pallas kernels  51.4 us (83%)
  local copies, waits for them, and re-layouts  6.16 us (10%)
  between operations  1.98 us (3%)
  other arithmetic  1.81 us (3%)
    pallas_call x1, Pallas kernels, gram_sums(): pl.pallas_call(functools.partial(gram_kernel, side), out_shape=jax.ShapeD...  51.4 us
    unnamed x8, local copies, waits for them, and re-layouts  2.97 us
    dynamic_slice x2, local copies, waits for them, and re-layouts, local(): damp = damp_levels[level_index[group]]  2.55 us
    add x1, other arithmetic, local(): return summed * col_mask + jnp.where(row_ids == col_ids, damp, 0.0)  1.79 us

profile of v1, /device:TPU:1, one launch (start us, length us, event | category | flops | bytes accessed | tf_op | source)
XLA Modules:
  0.0 61.3 jit_solution(7233909299187702322)
XLA Ops:
  0.0 0.0 copy-start
  0.0 1.2 %dynamic_slice.10 = s32[1]{0:T(128)} dynamic-slice(s32[8]{0:T(128)} %param.8, s32[]{:T(128)S(6)} %select_n.30), dynamic_slice_sizes={1} | dynamic-slice | bytes 12 | tf_op jit(solution)/shard_map/dynamic_slice | solution.py:256
  3.2 1.3 %dynamic_slice.11 = f32[1]{0:T(128)} dynamic-slice(f32[4]{0:T(128)} %param.9, s32[]{:T(128)S(6)} %select_n.33), dynamic_slice_sizes={1} | dynamic-slice | bytes 12 | tf_op jit(solution)/shard_map/dynamic_slice | solution.py:256
  4.5 0.0 copy-done
  4.5 0.6 %gather_fusion = s32[4]{0:T(128)S(1)} fusion(s32[8]{0:T(128)S(1)} %dynamic-slice_bitcast_fusion, s32[1024]{0:T(1024)S(1)} %pad_clamp_fusion), kind=kCustom, calls=%fused_computation | custom fusion | bytes 48 | tf_op jit(solution)/shard_map/gather | solution.py:255
  5.2 0.1 broadcast_bitcast_fusion
  5.3 0.0 copy-start.1
  5.3 2.2 %copy-done.1 = bf16[1024,2048]{1,0:T(8,128)(2,1)S(1)} copy-done((bf16[1024,2048]{1,0:T(8,128)(2,1)S(1)}, bf16[1024,2048]{1,0:T(8,128)(2,1)}, u32[]{:S(2)}) %copy-start.1) | copy-done | bytes 4194328
  7.5 0.0 copy-start.2
  7.5 0.7 %copy-done.2 = f32[2048]{0:T(1024)S(1)} copy-done((f32[2048]{0:T(1024)S(1)}, f32[2048]{0:T(1024)}, u32[]{:S(2)}) %copy-start.2) | copy-done | bytes 8216
  8.2 51.4 %shard_map.55 = f32[256,1024]{1,0:T(8,128)S(1)} custom-call(f32[1,2048]{1,0:T(1,128)S(1)} %bitcast.10, bf16[1024,2048]{1,0:T(8,128)(2,1)S(1)} %copy-done.1), custom_call_target="tpu_custom_call" | custom-call | flops 5368709120 | bytes 4194304 | tf_op jit(solution)/shard_map/pallas_call | solution.py:205
  59.5 1.8 %select_add_fusion = f32[256,1024]{1,0:T(8,128)} fusion(f32[256,1024]{1,0:T(8,128)S(1)} %shard_map.55, f32[]{:T(128)} %bitcast.4, s32[1024]{0:T(1024)S(1)} %iota_add_fusion, f32[1024]{0:T(1024)S(1)} %bitcast.11, s32[256]{0:T(256)S(1)} %iota_add_fusion.1), kind=kLoop, calls=%fused_computation.1 | loop fusion | flops 1048576 | bytes 2106372 | tf_op jit(solution)/shard_map/add | solution.py:260
  (7 shorter events, 0.0 us)
Async XLA Ops:
  0.0 4.5 %copy-start = (s32[8,8]{1,0:T(8,128)S(1)}, s32[8,8]{1,0:T(8,128)}, u32[]{:S(2)}) copy-start(s32[8,8]{1,0:T(8,128)} %param.7) | copy-start | bytes 772
  5.3 2.2 %copy-start.1 = (bf16[1024,2048]{1,0:T(8,128)(2,1)S(1)}, bf16[1024,2048]{1,0:T(8,128)(2,1)}, u32[]{:S(2)}) copy-start(bf16[1024,2048]{1,0:T(8,128)(2,1)} %s_ref.1) | copy-start | bytes 12582916
  7.5 0.7 %copy-start.2 = (f32[2048]{0:T(1024)S(1)}, f32[2048]{0:T(1024)}, u32[]{:S(2)}) copy-start(f32[2048]{0:T(1024)} %param.6) | copy-start | bytes 24580

commit v2 on v1

--- a/solution.py
+++ b/solution.py
@@ -36,7 +36,7 @@
 
 
 def gram_kernel(
-    side, w_ref, s_ref, out_ref,
+    side, w_ref, mask_ref, level_ref, damp_ref, s_ref, out_ref,
     sall, wgt, ysend, yrecv, zsend, zrecv, acc, msend, mrecv,
     load_sem, gsend_sem, grecv_sem, ysend_sem, yrecv_sem, zsend_sem, zrecv_sem, msend_sem, mrecv_sem,
 ):
@@ -70,14 +70,17 @@
             device_id={"tx": 1 - t}, device_id_type=MESH,
         )
 
+    def weigh(i):
+        load(i).wait()
+        rows = pl.ds(i * side, side)
+        wgt[rows, :] = (sall[0, rows, :].astype(jnp.float32) * w_ref[...]).astype(jnp.bfloat16)
+
+    weigh(0)
     pl.semaphore_wait(barrier, 15)
     for r in ((1 - y) + 2, 1 - y, y + 2, y):
         gather(r).start()
-
-    for i in range(4):
-        load(i).wait()
-        rows = pl.ds(i * side, side)
-        wgt[rows, :] = (sall[0, rows, :].astype(jnp.float32) * w_ref[...]).astype(jnp.bfloat16)
+    for i in range(1, 4):
+        weigh(i)
 
     def place(i, a):
         r = a + 2 * (i % 2)
@@ -148,6 +151,16 @@
     rank = c % 4
     same = c // 4 == t
 
+    mask_row = mask_ref[pl.ds(c, 1), :].astype(jnp.float32)
+    group_ids = lax.broadcasted_iota(jnp.int32, mask_row.shape, 1)
+    level = jnp.sum(jnp.where(group_ids == c, level_ref[...], 0), axis=1, keepdims=True)
+    level_ids = lax.broadcasted_iota(jnp.int32, damp_ref.shape, 1)
+    damp = jnp.sum(jnp.where(level_ids == level, damp_ref[...], 0.0), axis=1, keepdims=True)
+
+    def masked(q, total):
+        mask = jnp.sum(jnp.where(group_ids == 4 * t + q, mask_row, 0.0), axis=1, keepdims=True)
+        return total * mask
+
     def held(q):
         return jnp.where(same, q >= rank, q <= rank)
 
@@ -161,7 +174,13 @@
                 source = (z + k) % 4
                 zcopy(0, q, z, source).wait_recv()
                 total = total + read(zrecv.at[source, q])
-            out_ref[:, columns] = total
+            out_ref[:, columns] = masked(q, total)
+
+            @pl.when(jnp.logical_and(same, q == rank))
+            def _():
+                row_ids = lax.broadcasted_iota(jnp.int32, total.shape, 0)
+                col_ids = lax.broadcasted_iota(jnp.int32, total.shape, 1)
+                out_ref[:, columns] += jnp.where(row_ids == col_ids, damp, 0.0)
 
             @pl.when(q != rank)
             def _():
@@ -174,7 +193,7 @@
         @pl.when(jnp.logical_not(held(q)))
         def _():
             mcopy(q, q).wait_recv()
-            out_ref[:, columns] = read(mrecv.at[q]).T
+            out_ref[:, columns] = masked(q, read(mrecv.at[q]).T)
 
     for r in range(4):
         gather(r).wait_send()
@@ -196,7 +215,8 @@
             mcopy(q, rank).wait_send()
 
 
-def gram_sums(sensitivity, cell_weight, groups):
+def gram_tiles(sensitivity, cell_weight, pair_mask, level_index, damp_levels):
+    groups = pair_mask.shape[0]
     own_rows, cells = sensitivity.shape
     side = 2 * own_rows // groups
     tile = (side, side)
@@ -207,7 +227,10 @@
         out_shape=jax.ShapeDtypeStruct((side, own_rows), jnp.float32),
         in_specs=[
             pl.BlockSpec(memory_space=pltpu.VMEM),
-            pl.BlockSpec(memory_space=pl.ANY),
+            pl.BlockSpec(memory_space=pltpu.VMEM),
+            pl.BlockSpec(memory_space=pltpu.VMEM),
+            pl.BlockSpec(memory_space=pltpu.VMEM),
+            pl.BlockSpec(memory_space=pltpu.HBM),
         ],
         out_specs=pl.BlockSpec(memory_space=pltpu.VMEM),
         scratch_shapes=[
@@ -224,12 +247,12 @@
             dma((10,)), dma((10,)), dma((10,)), dma((4, 4)), dma((4,)), dma((4,)),
         ],
         compiler_params=pltpu.CompilerParams(
-            collective_id=0, has_side_effects=True, vmem_limit_bytes=48 * 1024 * 1024
+            collective_id=0, has_side_effects=True, vmem_limit_bytes=60 * 1024 * 1024
         ),
         cost_estimate=pl.CostEstimate(
             flops=2 * 20 * side * side * cells, bytes_accessed=own_rows * cells * 2, transcendentals=0
         ),
-    )(cell_weight[None, :], sensitivity)
+    )(cell_weight[None, :], pair_mask, level_index[None, :], damp_levels[None, :], sensitivity)
 
 
 def plain_sums(sensitivity, cell_weight):
@@ -247,9 +270,8 @@
     tx_pos = lax.axis_index("tx")
     cell_pos = lax.axis_index("cell")
     if lax.axis_size("tx") == 2 and lax.axis_size("cell") == 8 and groups == 8:
-        summed = gram_sums(sensitivity, cell_weight, groups)
-    else:
-        summed = plain_sums(sensitivity, cell_weight)
+        return gram_tiles(sensitivity, cell_weight, pair_mask, level_index, damp_levels)
+    summed = plain_sums(sensitivity, cell_weight)
     group = cell_pos * part_rows // group_rows
     col_groups = tx_pos * own_rows // group_rows + jnp.arange(own_rows // group_rows, dtype=jnp.int32)
     mask_row = pair_mask[group][col_groups].astype(jnp.float32)

time: 61.6 us -> 55.3 us (0.90)
  local copies, waits for them, and re-layouts: 6.16 us -> 2.31 us
  between operations: 1.98 us -> 0.01 us
  other arithmetic: 1.81 us -> 0 us
  Pallas kernels: 51.4 us -> 52.8 us
    dynamic_slice x2 -> x0, local copies, waits for them, and re-layouts: 2.55 us -> none  [local(): damp = damp_levels[level_index[group]]]
    add x3 -> x0, other arithmetic: 1.79 us -> none  [the longest x1 1.79 us: local(): return summed * col_mask + jnp.where(row_ids == col_ids, damp, 0.0)]
    pallas_call x1, Pallas kernels: 51.4 us -> 52.8 us  [gram_tiles(): pl.pallas_call(functools.partial(gram_kernel, side), out_shape=jax.ShapeD...]
    unnamed x8 -> x1, local copies, waits for them, and re-layouts: 2.97 us -> 2.31 us
    gather x1 -> x0, local copies, waits for them, and re-layouts: 0.64 us -> none  [local(): mask_row = pair_mask[group][col_groups].astype(jnp.float32)]
where the time goes in v2:
time: 55.3 us; the launch traced here: 55.1 us
  Pallas kernels  52.8 us (95%)
  local copies, waits for them, and re-layouts  2.31 us (4%)
    pallas_call x1, Pallas kernels, gram_tiles(): pl.pallas_call(functools.partial(gram_kernel, side), out_shape=jax.ShapeD...  52.8 us
    unnamed x1, local copies, waits for them, and re-layouts  2.31 us

profile of v2, /device:TPU:1, one launch (start us, length us, event | category | flops | bytes accessed | tf_op | source)
XLA Modules:
  0.0 55.1 jit_solution(5231531553810808057)
XLA Ops:
  0.0 52.8 %shard_map.55 = f32[256,1024]{1,0:T(8,128)} custom-call(f32[1,2048]{1,0:T(1,128)} %bitcast.3, s32[8,8]{1,0:T(8,128)} %mask_ref.1, s32[1,8]{1,0:T(1,128)} %bitcast.4, f32[1,4]{1,0:T(1,128)} %bitcast.5, bf16[1024,2048]{1,0:T(8,128)(2,1)} %s_ref.1), custom_call_target="tpu_custom_call" | custom-call | flops 5368709120 | bytes 4194304 | tf_op jit(solution)/shard_map/pallas_call | solution.py:225
  52.8 2.3 %copy.7 = f32[256,1024]{1,0:T(8,128)} copy(f32[256,1024]{1,0:T(8,128)} %shard_map.55) | data formatting | bytes 2097152

commit v3 on v2

--- a/solution.py
+++ b/solution.py
@@ -37,12 +37,17 @@
 
 def gram_kernel(
     side, w_ref, mask_ref, level_ref, damp_ref, s_ref, out_ref,
-    sall, wgt, ysend, yrecv, zsend, zrecv, acc, msend, mrecv,
-    load_sem, gsend_sem, grecv_sem, ysend_sem, yrecv_sem, zsend_sem, zrecv_sem, msend_sem, mrecv_sem,
+    sall, wgt, ysend, yrecv, yhsend, yhrecv, zsend, zrecv, zhsend, zhrecv,
+    acc, hacc, msend, mrecv, mhsend, mhrecv,
+    load_sem, gsend_sem, grecv_sem, ysend_sem, yrecv_sem, zsend_sem, zrecv_sem, zhrecv_sem,
+    msend_sem, mrecv_sem, mhsend_sem, mhrecv_sem,
 ):
     t = lax.axis_index("tx")
     c = lax.axis_index("cell")
     z, y = c // 2, c % 2
+    rank = c % 4
+    same = c // 4 == t
+    half_side = side // 2
 
     def block(r):
         return pl.ds(pl.multiple_of(r * side, side), side)
@@ -52,7 +57,7 @@
             s_ref.at[pl.ds(i * side, side), :], sall.at[0, pl.ds(i * side, side), :], load_sem.at[i]
         )
 
-    for i in range(4):
+    for i in (1, 2, 3, 0):
         load(i).start()
 
     barrier = pltpu.get_barrier_semaphore()
@@ -71,85 +76,134 @@
         )
 
     def weigh(i):
-        load(i).wait()
         rows = pl.ds(i * side, side)
         wgt[rows, :] = (sall[0, rows, :].astype(jnp.float32) * w_ref[...]).astype(jnp.bfloat16)
 
-    weigh(0)
+    def place(i, a):
+        near = i < 4
+        ri = jnp.where(near, i // 2, i % 2)
+        e = jnp.where(near, 1 + i % 2, jnp.where(i < 6, 3, jnp.where(i < 8, 4, 0)))
+        r = a + 2 * ri
+        return r, e, (r + e) % 4, (r + e) // 4
+
+    def product(i, a):
+        r, e, q, half = place(i, a)
+
+        @pl.when(r + e == 4)
+        def _():
+            gather(r).wait_recv()
+
+        return contract(sall[half, block(r), :], wgt[block(q), :])
+
+    def half_product(i, a, ref):
+        r, e, q, half = place(i, a)
+
+        @pl.when(r + e == 4)
+        def _():
+            gather(r).wait_recv()
+
+        upper = (t + half) % 2
+        for u in range(2):
+            v = (u + upper) % 2
+            rows = pl.ds(pl.multiple_of(r * side + u * half_side, half_side), half_side)
+            cols = pl.ds(pl.multiple_of(q * side + v * half_side, half_side), half_side)
+            ref[u * half_side:(u + 1) * half_side, :] = contract(sall[half, rows, :], wgt[cols, :])
+
+    def ycopy(i, halved):
+        src, dst = (yhsend.at[i - 6], yhrecv.at[i - 6]) if halved else (ysend.at[i], yrecv.at[i])
+        return pltpu.make_async_remote_copy(
+            src_ref=src, dst_ref=dst,
+            send_sem=ysend_sem.at[i], recv_sem=yrecv_sem.at[i],
+            device_id={"cell": 2 * z + 1 - y}, device_id_type=MESH,
+        )
+
+    def zcopy(i, q, owner, source, halved):
+        src, dst = (zhsend.at[i - 6], zhrecv.at[source]) if halved else (zsend.at[i], zrecv.at[source, q])
+        return pltpu.make_async_remote_copy(
+            src_ref=src, dst_ref=dst,
+            send_sem=zsend_sem.at[i], recv_sem=zhrecv_sem.at[source] if halved else zrecv_sem.at[source, q],
+            device_id={"cell": 2 * owner + y}, device_id_type=MESH,
+        )
+
+    def mcopy(q, slot):
+        return pltpu.make_async_remote_copy(
+            src_ref=msend.at[q], dst_ref=mrecv.at[slot],
+            send_sem=msend_sem.at[q], recv_sem=mrecv_sem.at[slot],
+            device_id={"cell": 4 * t + q, "tx": c // 4}, device_id_type=MESH,
+        )
+
+    def mhcopy():
+        return pltpu.make_async_remote_copy(
+            src_ref=mhsend, dst_ref=mhrecv,
+            send_sem=mhsend_sem.at[0], recv_sem=mhrecv_sem.at[0],
+            device_id={"cell": 4 * t + rank, "tx": 1 - t}, device_id_type=MESH,
+        )
+
+    def send(i, carry):
+        write(ysend.at[i], product(i, 1 - y))
+        ycopy(i, False).start()
+        return carry
+
+    def send_half(i, carry):
+        half_product(i, 1 - y, hacc.at[1])
+        write(yhsend.at[i - 6], hacc[1])
+        ycopy(i, True).start()
+        return carry
+
+    def owner_of(i):
+        r, e, q, half = place(i, y)
+        return q, 2 * ((t + half) % 2) + r // 2
+
+    def keep(i, carry):
+        q, owner = owner_of(i)
+        part = product(i, y)
+        ycopy(i, False).wait_recv()
+        part = part + read(yrecv.at[i])
+
+        @pl.when(owner == z)
+        def _():
+            acc[q] = part
+
+        @pl.when(owner != z)
+        def _():
+            write(zsend.at[i], part)
+            zcopy(i, q, owner, z, False).start()
+
+        return carry
+
+    def keep_half(i, carry):
+        q, owner = owner_of(i)
+        half_product(i, y, hacc.at[1])
+        ycopy(i, True).wait_recv()
+        part = hacc[1] + read(yhrecv.at[i - 6])
+
+        @pl.when(owner == z)
+        def _():
+            hacc[0] = part
+
+        @pl.when(owner != z)
+        def _():
+            write(zhsend.at[i - 6], part)
+            zcopy(i, q, owner, z, True).start()
+
+        return carry
+
+    load(1).wait()
+    weigh(1)
+    load(2).wait()
+    weigh(2)
+    load(3).wait()
+    load(0).wait()
     pl.semaphore_wait(barrier, 15)
     for r in ((1 - y) + 2, 1 - y, y + 2, y):
         gather(r).start()
-    for i in range(1, 4):
-        weigh(i)
-
-    def place(i, a):
-        r = a + 2 * (i % 2)
-        e = i // 2
-        half = (r + e) // 4
-        return r, (r + e) % 4, half, r + e == 4
-
-    def product(i, a):
-        r, q, half, first = place(i, a)
-
-        @pl.when(first)
-        def _():
-            gather(r).wait_recv()
-
-        return contract(sall[half, block(r), :], wgt[block(q), :])
-
-    def ycopy(i):
-        return pltpu.make_async_remote_copy(
-            src_ref=ysend.at[i], dst_ref=yrecv.at[i],
-            send_sem=ysend_sem.at[i], recv_sem=yrecv_sem.at[i],
-            device_id={"cell": 2 * z + 1 - y}, device_id_type=MESH,
-        )
-
-    def zcopy(i, q, owner, source):
-        return pltpu.make_async_remote_copy(
-            src_ref=zsend.at[i], dst_ref=zrecv.at[source, q],
-            send_sem=zsend_sem.at[i], recv_sem=zrecv_sem.at[source, q],
-            device_id={"cell": 2 * owner + y}, device_id_type=MESH,
-        )
-
-    def mcopy(q, slot):
-        return pltpu.make_async_remote_copy(
-            src_ref=msend.at[q], dst_ref=mrecv.at[slot],
-            send_sem=msend_sem.at[q], recv_sem=mrecv_sem.at[slot],
-            device_id={"cell": 4 * t + q, "tx": c // 4}, device_id_type=MESH,
-        )
-
-    def first_phase(i, carry):
-        write(ysend.at[i], product(i, 1 - y))
-        ycopy(i).start()
-        return carry
-
-    lax.fori_loop(0, 10, first_phase, 0)
-
-    def owner_of(i):
-        r, q, half, _ = place(i, y)
-        return q, 2 * ((t + half) % 2) + r // 2
-
-    def second_phase(i, carry):
-        q, owner = owner_of(i)
-        part = product(i, y)
-        ycopy(i).wait_recv()
-        part = part + read(yrecv.at[i])
-
-        @pl.when(owner == z)
-        def _():
-            acc[q] = part
-
-        @pl.when(owner != z)
-        def _():
-            write(zsend.at[i], part)
-            zcopy(i, q, owner, z).start()
-
-        return carry
-
-    lax.fori_loop(0, 10, second_phase, 0)
-
-    rank = c % 4
-    same = c // 4 == t
+    lax.fori_loop(0, 1, send, 0)
+    weigh(3)
+    lax.fori_loop(1, 2, send, 0)
+    weigh(0)
+    lax.fori_loop(2, 6, send, 0)
+    lax.fori_loop(6, 8, send_half, 0)
+    lax.fori_loop(8, 10, send, 0)
 
     mask_row = mask_ref[pl.ds(c, 1), :].astype(jnp.float32)
     group_ids = lax.broadcasted_iota(jnp.int32, mask_row.shape, 1)
@@ -161,58 +215,100 @@
         mask = jnp.sum(jnp.where(group_ids == 4 * t + q, mask_row, 0.0), axis=1, keepdims=True)
         return total * mask
 
-    def held(q):
-        return jnp.where(same, q >= rank, q <= rank)
+    def distance(q):
+        return (4 * t + q - c + 8) % 8
+
+    def summed(q):
+        total = acc[q]
+        for k in range(1, 4):
+            source = (z + k) % 4
+            zcopy(0, q, z, source, False).wait_recv()
+            total = total + read(zrecv.at[source, q])
+        return total
+
+    def mirrored(q):
+        return jnp.logical_and(distance(q) >= 1, distance(q) <= 3)
+
+    lax.fori_loop(0, 6, keep, 0)
+    lax.fori_loop(6, 8, keep_half, 0)
 
     for q in range(4):
-        columns = pl.ds(q * side, side)
-
-        @pl.when(held(q))
-        def _():
-            total = acc[q]
-            for k in range(1, 4):
-                source = (z + k) % 4
-                zcopy(0, q, z, source).wait_recv()
-                total = total + read(zrecv.at[source, q])
-            out_ref[:, columns] = masked(q, total)
-
-            @pl.when(jnp.logical_and(same, q == rank))
-            def _():
-                row_ids = lax.broadcasted_iota(jnp.int32, total.shape, 0)
-                col_ids = lax.broadcasted_iota(jnp.int32, total.shape, 1)
-                out_ref[:, columns] += jnp.where(row_ids == col_ids, damp, 0.0)
-
-            @pl.when(q != rank)
-            def _():
-                write(msend.at[q], total)
-                mcopy(q, rank).start()
+        @pl.when(mirrored(q))
+        def _():
+            total = summed(q)
+            write(msend.at[q], total)
+            mcopy(q, rank).start()
+            out_ref[:, pl.ds(q * side, side)] = masked(q, total)
+
+    def quarter(u, v):
+        return (
+            pl.ds(u * half_side, half_side) if isinstance(u, int)
+            else pl.ds(pl.multiple_of(u * half_side, half_side), half_side),
+            pl.ds(pl.multiple_of(rank * side + v * half_side, half_side), half_side),
+        )
+
+    @pl.when(jnp.logical_not(same))
+    def _():
+        total = hacc[0]
+        for k in range(1, 4):
+            source = (z + k) % 4
+            zcopy(6, 0, z, source, True).wait_recv()
+            total = total + read(zhrecv.at[source])
+        write(mhsend, total)
+        mhcopy().start()
+        total = masked(rank, total)
+        for u in range(2):
+            rows, cols = quarter(u, (u + c // 4) % 2)
+            out_ref[rows, cols] = total[u * half_side:(u + 1) * half_side, :]
+
+    lax.fori_loop(8, 10, keep, 0)
 
     for q in range(4):
-        columns = pl.ds(q * side, side)
-
-        @pl.when(jnp.logical_not(held(q)))
+        @pl.when(distance(q) >= 5)
         def _():
             mcopy(q, q).wait_recv()
-            out_ref[:, columns] = masked(q, read(mrecv.at[q]).T)
+            out_ref[:, pl.ds(q * side, side)] = masked(q, read(mrecv.at[q]).T)
+
+    @pl.when(jnp.logical_not(same))
+    def _():
+        mhcopy().wait_recv()
+        total = masked(rank, read(mhrecv))
+        for u in range(2):
+            v = (u + 1 - c // 4) % 2
+            rows, cols = quarter(v, u)
+            out_ref[rows, cols] = total[u * half_side:(u + 1) * half_side, :].T
+
+    @pl.when(same)
+    def _():
+        total = masked(rank, summed(rank))
+        row_ids = lax.broadcasted_iota(jnp.int32, total.shape, 0)
+        col_ids = lax.broadcasted_iota(jnp.int32, total.shape, 1)
+        out_ref[:, block(rank)] = total + jnp.where(row_ids == col_ids, damp, 0.0)
 
     for r in range(4):
         gather(r).wait_send()
 
-    def drain(i, carry):
-        ycopy(i).wait_send()
+    def drain(halved, i, carry):
+        ycopy(i, halved).wait_send()
         q, owner = owner_of(i)
 
         @pl.when(owner != z)
         def _():
-            zcopy(i, q, owner, z).wait_send()
-
-        return carry
-
-    lax.fori_loop(0, 10, drain, 0)
+            zcopy(i, q, owner, z, halved).wait_send()
+
+        return carry
+
+    lax.fori_loop(0, 6, functools.partial(drain, False), 0)
+    lax.fori_loop(6, 8, functools.partial(drain, True), 0)
+    lax.fori_loop(8, 10, functools.partial(drain, False), 0)
     for q in range(4):
-        @pl.when(jnp.logical_and(held(q), q != rank))
+        @pl.when(mirrored(q))
         def _():
             mcopy(q, rank).wait_send()
+
+    @pl.when(jnp.logical_not(same))
+    def _():
+        mhcopy().wait_send()
 
 
 def gram_tiles(sensitivity, cell_weight, pair_mask, level_index, damp_levels):
@@ -221,6 +317,7 @@
     side = 2 * own_rows // groups
     tile = (side, side)
     wire = (side + HEAD, side)
+    slim = (side + HEAD, side // 2)
     dma = pltpu.SemaphoreType.DMA
     return pl.pallas_call(
         functools.partial(gram_kernel, side),
@@ -238,13 +335,21 @@
             pltpu.VMEM((own_rows, cells), jnp.bfloat16),
             pltpu.VMEM((10,) + wire, WIRE),
             pltpu.VMEM((10,) + wire, WIRE),
+            pltpu.VMEM((2,) + slim, WIRE),
+            pltpu.VMEM((2,) + slim, WIRE),
             pltpu.VMEM((10,) + wire, WIRE),
             pltpu.VMEM((4, 4) + wire, WIRE),
+            pltpu.VMEM((2,) + slim, WIRE),
+            pltpu.VMEM((4,) + slim, WIRE),
             pltpu.VMEM((4,) + tile, jnp.float32),
+            pltpu.VMEM((2, side, side // 2), jnp.float32),
             pltpu.VMEM((4,) + wire, WIRE),
             pltpu.VMEM((4,) + wire, WIRE),
+            pltpu.VMEM(slim, WIRE),
+            pltpu.VMEM(slim, WIRE),
             dma((4,)), dma((4,)), dma((4,)),
-            dma((10,)), dma((10,)), dma((10,)), dma((4, 4)), dma((4,)), dma((4,)),
+            dma((10,)), dma((10,)), dma((10,)), dma((4, 4)), dma((4,)),
+            dma((4,)), dma((4,)), dma((1,)), dma((1,)),
         ],
         compiler_params=pltpu.CompilerParams(
             collective_id=0, has_side_effects=True, vmem_limit_bytes=60 * 1024 * 1024

time: 55.3 us -> 58.9 us (1.065)
  the two profiles are of different devices: /device:TPU:1 before, /device:TPU:31 now
where the time goes in v3:
time: 58.9 us; the launch traced here: 58.7 us
  Pallas kernels  56.4 us (96%)
  local copies, waits for them, and re-layouts  2.31 us (4%)
    pallas_call x1, Pallas kernels, gram_tiles(): pl.pallas_call(functools.partial(gram_kernel, side), out_shape=jax.ShapeD...  56.4 us
    unnamed x1, local copies, waits for them, and re-layouts  2.31 us

profile of v3, /device:TPU:31, one launch (start us, length us, event | category | flops | bytes accessed | tf_op | source)
XLA Modules:
  0.0 58.7 jit_solution(2127625547277533666)
XLA Ops:
  0.0 56.4 %shard_map.55 = f32[256,1024]{1,0:T(8,128)} custom-call(f32[1,2048]{1,0:T(1,128)} %bitcast.3, s32[8,8]{1,0:T(8,128)} %mask_ref.1, s32[1,8]{1,0:T(1,128)} %bitcast.4, f32[1,4]{1,0:T(1,128)} %bitcast.5, bf16[1024,2048]{1,0:T(8,128)(2,1)} %s_ref.1), custom_call_target="tpu_custom_call" | custom-call | flops 5368709120 | bytes 4194304 | tf_op jit(solution)/shard_map/pallas_call | solution.py:322
  56.4 2.3 %copy.7 = f32[256,1024]{1,0:T(8,128)} copy(f32[256,1024]{1,0:T(8,128)} %shard_map.55) | data formatting | bytes 2097152

commit v4 on v2

v4 whole, which is shorter than its diff:
```python
import functools

import jax
import jax.numpy as jnp
from jax import lax
from jax.experimental import pallas as pl
from jax.experimental.pallas import tpu as pltpu
from jax.sharding import PartitionSpec as P

MESH = pl.DeviceIdType.MESH
WIRE = jnp.int16
TOP = 32752.0
HEAD = 16
DISTANCES = (1, 2, 3, 4, 0)


def contract(left, right):
    return lax.dot_general(
        left, right, (((1,), (1,)), ((), ())), preferred_element_type=jnp.float32
    )


def write(ref, value):
    side = value.shape[0]
    peak = jnp.maximum(jnp.max(jnp.abs(value), axis=0, keepdims=True), 2.0**-60)
    power = jnp.ceil(jnp.log2(peak))
    ref[pl.ds(0, side), :] = jnp.round(value * (jnp.exp2(-power) * TOP)).astype(jnp.int32).astype(WIRE)
    head = jnp.broadcast_to(power.astype(jnp.int32), (HEAD, value.shape[1]))
    ref[pl.ds(side, HEAD), :] = head.astype(WIRE)


def read(ref):
    side = ref.shape[0] - HEAD
    power = ref[pl.ds(side, HEAD), :].astype(jnp.int32).astype(jnp.float32)[:1, :]
    whole = ref[pl.ds(0, side), :].astype(jnp.int32).astype(jnp.float32)
    return whole * (jnp.exp2(power) * (1.0 / TOP))


def gram_kernel(side, w_ref, mask_ref, level_ref, damp_ref, s_ref, out_ref, sall, wgt, *refs):
    ysend, yrecv, near_send, near_recv, far_send, far_recv, acc, msend, mrecv = (
        refs[n * 5:n * 5 + 5] for n in range(9)
    )
    (load_sem, gsend_sem, grecv_sem, ysend_sem, yrecv_sem, near_send_sem, near_recv_sem,
     far_send_sem, far_recv_sem, msend_sem, mrecv_sem) = refs[45:]
    t = lax.axis_index("tx")
    c = lax.axis_index("cell")
    z, y = c // 2, c % 2
    rank, upper, zb = c % 4, c // 4, z % 2
    half_side = side // 2

    def block(r):
        return pl.ds(pl.multiple_of(r * side, side), side)

    def load(i):
        return pltpu.make_async_copy(
            s_ref.at[pl.ds(i * side, side), :], sall.at[0, pl.ds(i * side, side), :], load_sem.at[i]
        )

    for i in range(4):
        load(i).start()

    barrier = pltpu.get_barrier_semaphore()
    for k in range(1, 16):
        pl.semaphore_signal(
            barrier, inc=1,
            device_id={"tx": (t + k // 8) % 2, "cell": (c + k % 8) % 8},
            device_id_type=MESH,
        )

    def remote(src, dst, send_sem, recv_sem, device):
        return pltpu.make_async_remote_copy(
            src_ref=src, dst_ref=dst, send_sem=send_sem, recv_sem=recv_sem,
            device_id=device, device_id_type=MESH,
        )

    def gather(r):
        return remote(
            s_ref.at[block(r), :], sall.at[1, block(r), :], gsend_sem.at[r], grecv_sem.at[r], {"tx": 1 - t}
        )

    def ycopy(k, s):
        return remote(
            ysend[k].at[s], yrecv[k].at[s], ysend_sem.at[2 * k + s], yrecv_sem.at[2 * k + s],
            {"cell": 2 * z + 1 - y},
        )

    def near_copy(k):
        return remote(
            near_send[k], near_recv[k], near_send_sem.at[k], near_recv_sem.at[k],
            {"cell": 2 * (z + 1 - 2 * zb) + y},
        )

    def far_copy(k):
        return remote(
            far_send[k], far_recv[k], far_send_sem.at[k], far_recv_sem.at[k], {"cell": (c + 4) % 8}
        )

    def mcopy(k):
        return remote(
            msend[k], mrecv[k], msend_sem.at[k], mrecv_sem.at[k],
            {"cell": (c + DISTANCES[k]) % 8, "tx": upper},
        )

    def weigh(i):
        rows = block(i)
        wgt[rows, :] = (sall[0, rows, :].astype(jnp.float32) * w_ref[...]).astype(jnp.bfloat16)

    def product(e, r):
        half, q = (r + e) // 4, (r + e) % 4
        if e:
            @pl.when(r + e == 4)
            def _():
                gather(r).wait_recv()
        if e != 4:
            return contract(sall[half, block(r), :], wgt[block(q), :])
        quarters = []
        for u in range(2):
            v = (u + t + half) % 2
            rows = pl.ds(pl.multiple_of(r * side + u * half_side, half_side), half_side)
            cols = pl.ds(pl.multiple_of(q * side + v * half_side, half_side), half_side)
            quarters.append(contract(sall[half, rows, :], wgt[cols, :]))
        return jnp.concatenate(quarters, axis=0)

    for i in range(4):
        load(i).wait()
    first = 1 - y + 2 * (1 - zb)
    weigh((first + 1) % 4)
    pl.semaphore_wait(barrier, 15)
    for r in ((1 - y) + 2, 1 - y, y + 2, y):
        gather(r).start()

    for k, e in enumerate(DISTANCES):
        for s in range(2):
            write(ysend[k].at[s], product(e, (first + 2 * s) % 4))
            ycopy(k, s).start()
            if k == 0:
                weigh((first + 3 - s) % 4)
            elif k == 1 and s == 0:
                weigh(first % 4)

    mask_row = mask_ref[pl.ds(c, 1), :].astype(jnp.float32)
    group_ids = lax.broadcasted_iota(jnp.int32, mask_row.shape, 1)
    level = jnp.sum(jnp.where(group_ids == c, level_ref[...], 0), axis=1, keepdims=True)
    level_ids = lax.broadcasted_iota(jnp.int32, damp_ref.shape, 1)
    damp = jnp.sum(jnp.where(level_ids == level, damp_ref[...], 0.0), axis=1, keepdims=True)

    def masked(q, total):
        mask = jnp.sum(jnp.where(group_ids == 4 * t + q, mask_row, 0.0), axis=1, keepdims=True)
        return total * mask

    def held(e):
        return (t + (rank + e) // 4) % 2 == upper

    def quarter(u, v):
        q = pl.multiple_of(rank * side + v * half_side, half_side)
        return pl.ds(pl.multiple_of(u * half_side, half_side), half_side), pl.ds(q, half_side)

    def over_y(k, e):
        part = product(e, (rank + 2) % 4)
        ycopy(k, 0).wait_recv()
        write(near_send[k], part + read(yrecv[k].at[0]))
        near_copy(k).start()
        part = product(e, rank)
        ycopy(k, 1).wait_recv()
        acc[k][...] = part + read(yrecv[k].at[1])

    def over_near(k, e):
        near_copy(k).wait_recv()
        part = acc[k][...] + read(near_recv[k])

        @pl.when(held(e))
        def _():
            acc[k][...] = part

        @pl.when(jnp.logical_not(held(e)))
        def _():
            write(far_send[k], part)
            far_copy(k).start()

    def over_far(k, e):
        @pl.when(held(e))
        def _():
            far_copy(k).wait_recv()
            total = acc[k][...] + read(far_recv[k])
            if e:
                write(msend[k], total)
                mcopy(k).start()
            q = (rank + e) % 4
            total = masked(q, total)
            if e == 0:
                row_ids = lax.broadcasted_iota(jnp.int32, total.shape, 0)
                col_ids = lax.broadcasted_iota(jnp.int32, total.shape, 1)
                total = total + jnp.where(row_ids == col_ids, damp, 0.0)
            if e != 4:
                out_ref[:, block(q)] = total
            else:
                for u in range(2):
                    rows, cols = quarter(u, (u + upper) % 2)
                    out_ref[rows, cols] = total[u * half_side:(u + 1) * half_side, :]

    def mirror(k, e):
        @pl.when((c + 8 - e) % 8 // 4 == t)
        def _():
            mcopy(k).wait_recv()
            q = (rank + 4 - e) % 4
            total = masked(q, read(mrecv[k]))
            if e != 4:
                out_ref[:, block(q)] = total.T
            else:
                for u in range(2):
                    rows, cols = quarter((u + 1 - upper) % 2, u)
                    out_ref[rows, cols] = total[u * half_side:(u + 1) * half_side, :].T

    steps = (over_y, over_near, over_far)
    for now in range(len(DISTANCES) + 2):
        for lag, step in enumerate(steps):
            if 0 <= now - lag < len(DISTANCES):
                step(now - lag, DISTANCES[now - lag])
    for k, e in enumerate(DISTANCES):
        if e:
            mirror(k, e)

    for r in range(4):
        gather(r).wait_send()
    for k, e in enumerate(DISTANCES):
        for s in range(2):
            ycopy(k, s).wait_send()
        near_copy(k).wait_send()

        @pl.when(jnp.logical_not(held(e)))
        def _():
            far_copy(k).wait_send()

        if e:
            @pl.when(held(e))
            def _():
                mcopy(k).wait_send()


def gram_tiles(sensitivity, cell_weight, pair_mask, level_index, damp_levels):
    groups = pair_mask.shape[0]
    own_rows, cells = sensitivity.shape
    side = 2 * own_rows // groups
    widths = [side // 2 if e == 4 else side for e in DISTANCES]

    def wire(*lead):
        return [pltpu.VMEM(lead + (side + HEAD, width), WIRE) for width in widths]

    dma = pltpu.SemaphoreType.DMA
    return pl.pallas_call(
        functools.partial(gram_kernel, side),
        out_shape=jax.ShapeDtypeStruct((side, own_rows), jnp.float32),
        in_specs=[
            pl.BlockSpec(memory_space=pltpu.VMEM),
            pl.BlockSpec(memory_space=pltpu.VMEM),
            pl.BlockSpec(memory_space=pltpu.VMEM),
            pl.BlockSpec(memory_space=pltpu.VMEM),
            pl.BlockSpec(memory_space=pltpu.HBM),
        ],
        out_specs=pl.BlockSpec(memory_space=pltpu.VMEM),
        scratch_shapes=[
            pltpu.VMEM((2, own_rows, cells), jnp.bfloat16),
            pltpu.VMEM((own_rows, cells), jnp.bfloat16),
            *wire(2), *wire(2), *wire(), *wire(), *wire(), *wire(),
            *[pltpu.VMEM((side, width), jnp.float32) for width in widths],
            *wire(), *wire(),
            dma((4,)), dma((4,)), dma((4,)),
            dma((10,)), dma((10,)), dma((5,)), dma((5,)), dma((5,)), dma((5,)), dma((5,)), dma((5,)),
        ],
        compiler_params=pltpu.CompilerParams(
            collective_id=0, has_side_effects=True, vmem_limit_bytes=60 * 1024 * 1024
        ),
        cost_estimate=pl.CostEstimate(
            flops=2 * 20 * side * side * cells, bytes_accessed=own_rows * cells * 2, transcendentals=0
        ),
    )(cell_weight[None, :], pair_mask, level_index[None, :], damp_levels[None, :], sensitivity)


def plain_sums(sensitivity, cell_weight):
    weighted = (sensitivity.astype(jnp.float32) * cell_weight[None, :]).astype(jnp.bfloat16)
    everyone = lax.all_gather(sensitivity, "tx", axis=0, tiled=True)
    return lax.psum_scatter(contract(everyone, weighted), "cell", scatter_dimension=0, tiled=True)


def local(sensitivity, cell_weight, pair_mask, level_index, damp_levels):
    own_rows = sensitivity.shape[0]
    groups = pair_mask.shape[0]
    total_rows = own_rows * lax.axis_size("tx")
    part_rows = total_rows // lax.axis_size("cell")
    group_rows = total_rows // groups
    tx_pos = lax.axis_index("tx")
    cell_pos = lax.axis_index("cell")
    if lax.axis_size("tx") == 2 and lax.axis_size("cell") == 8 and groups == 8:
        return gram_tiles(sensitivity, cell_weight, pair_mask, level_index, damp_levels)
    summed = plain_sums(sensitivity, cell_weight)
    group = cell_pos * part_rows // group_rows
    col_groups = tx_pos * own_rows // group_rows + jnp.arange(own_rows // group_rows, dtype=jnp.int32)
    mask_row = pair_mask[group][col_groups].astype(jnp.float32)
    damp = damp_levels[level_index[group]]
    row_ids = cell_pos * part_rows + lax.broadcasted_iota(jnp.int32, summed.shape, 0)
    col_ids = tx_pos * own_rows + lax.broadcasted_iota(jnp.int32, summed.shape, 1)
    col_mask = jnp.repeat(mask_row, group_rows)[None, :]
    return summed * col_mask + jnp.where(row_ids == col_ids, damp, 0.0)


def solution(mesh):
    in_specs = (P(("dom", "tx"), "cell"), P(("dom", "cell")), P("dom", None), P("dom"), P("dom"))
    out_specs = P(("dom", "cell"), "tx")
    return jax.shard_map(local, mesh=mesh, in_specs=in_specs, out_specs=out_specs, check_vma=False)
```

time: 55.3 us -> 55 us (level)
  the two profiles are of different devices: /device:TPU:1 before, /device:TPU:5 now
where the time goes in v4:
time: 55 us; the launch traced here: 54.8 us
  Pallas kernels  52.4 us (95%)
  local copies, waits for them, and re-layouts  2.31 us (4%)
    pallas_call x1, Pallas kernels, gram_tiles(): pl.pallas_call(functools.partial(gram_kernel, side), out_shape=jax.ShapeD...  52.4 us
    unnamed x1, local copies, waits for them, and re-layouts  2.31 us

profile of v4, /device:TPU:5, one launch (start us, length us, event | category | flops | bytes accessed | tf_op | source)
XLA Modules:
  0.0 54.8 jit_solution(16724012145900246450)
XLA Ops:
  0.0 52.4 %shard_map.55 = f32[256,1024]{1,0:T(8,128)} custom-call(f32[1,2048]{1,0:T(1,128)} %bitcast.3, s32[8,8]{1,0:T(8,128)} %mask_ref.1, s32[1,8]{1,0:T(1,128)} %bitcast.4, f32[1,4]{1,0:T(1,128)} %bitcast.5, bf16[1024,2048]{1,0:T(8,128)(2,1)} %s_ref.1), custom_call_target="tpu_custom_call" | custom-call | flops 5368709120 | bytes 4194304 | tf_op jit(solution)/shard_map/pallas_call | solution.py:250
  52.4 2.3 %copy.7 = f32[256,1024]{1,0:T(8,128)} copy(f32[256,1024]{1,0:T(8,128)} %shard_map.55) | data formatting | bytes 2097152

commit v5 on v4

--- a/solution.py
+++ b/solution.py
@@ -155,11 +155,13 @@
         q = pl.multiple_of(rank * side + v * half_side, half_side)
         return pl.ds(pl.multiple_of(u * half_side, half_side), half_side), pl.ds(q, half_side)
 
-    def over_y(k, e):
+    def over_y_first(k, e):
         part = product(e, (rank + 2) % 4)
         ycopy(k, 0).wait_recv()
         write(near_send[k], part + read(yrecv[k].at[0]))
         near_copy(k).start()
+
+    def over_y_second(k, e):
         part = product(e, rank)
         ycopy(k, 1).wait_recv()
         acc[k][...] = part + read(yrecv[k].at[1])
@@ -211,14 +213,17 @@
                     rows, cols = quarter((u + 1 - upper) % 2, u)
                     out_ref[rows, cols] = total[u * half_side:(u + 1) * half_side, :].T
 
-    steps = (over_y, over_near, over_far)
-    for now in range(len(DISTANCES) + 2):
-        for lag, step in enumerate(steps):
-            if 0 <= now - lag < len(DISTANCES):
-                step(now - lag, DISTANCES[now - lag])
+    last = len(DISTANCES) - 1
+    for k, e in enumerate(DISTANCES):
+        over_y_first(k, e)
+        if k:
+            over_far(k - 1, DISTANCES[k - 1])
+        over_y_second(k, e)
+        over_near(k, e)
     for k, e in enumerate(DISTANCES):
         if e:
             mirror(k, e)
+    over_far(last, DISTANCES[last])
 
     for r in range(4):
         gather(r).wait_send()

time: 55 us -> 60.1 us (1.093)
  the two profiles are of different devices: /device:TPU:5 before, /device:TPU:0 now
where the time goes in v5:
time: 60.1 us; the launch traced here: 59.9 us
  Pallas kernels  57.6 us (96%)
  local copies, waits for them, and re-layouts  2.31 us (4%)
    pallas_call x1, Pallas kernels, gram_tiles(): pl.pallas_call(functools.partial(gram_kernel, side), out_shape=jax.ShapeD...  57.6 us
    unnamed x1, local copies, waits for them, and re-layouts  2.31 us

profile of v5, /device:TPU:0, one launch (start us, length us, event | category | flops | bytes accessed | tf_op | source)
XLA Modules:
  0.0 59.9 jit_solution(8807280936735636189)
XLA Ops:
  0.0 57.6 %shard_map.55 = f32[256,1024]{1,0:T(8,128)} custom-call(f32[1,2048]{1,0:T(1,128)} %bitcast.3, s32[8,8]{1,0:T(8,128)} %mask_ref.1, s32[1,8]{1,0:T(1,128)} %bitcast.4, f32[1,4]{1,0:T(1,128)} %bitcast.5, bf16[1024,2048]{1,0:T(8,128)(2,1)} %s_ref.1), custom_call_target="tpu_custom_call" | custom-call | flops 5368709120 | bytes 4194304 | tf_op jit(solution)/shard_map/pallas_call | solution.py:255
  57.6 2.3 %copy.7 = f32[256,1024]{1,0:T(8,128)} copy(f32[256,1024]{1,0:T(8,128)} %shard_map.55) | data formatting | bytes 2097152

commit v6 on v4

--- a/solution.py
+++ b/solution.py
@@ -129,7 +129,7 @@
     for r in ((1 - y) + 2, 1 - y, y + 2, y):
         gather(r).start()
 
-    for k, e in enumerate(DISTANCES):
+    def send_y(k, e):
         for s in range(2):
             write(ysend[k].at[s], product(e, (first + 2 * s) % 4))
             ycopy(k, s).start()
@@ -137,6 +137,9 @@
                 weigh((first + 3 - s) % 4)
             elif k == 1 and s == 0:
                 weigh(first % 4)
+
+    for k in range(2):
+        send_y(k, DISTANCES[k])
 
     mask_row = mask_ref[pl.ds(c, 1), :].astype(jnp.float32)
     group_ids = lax.broadcasted_iota(jnp.int32, mask_row.shape, 1)
@@ -216,6 +219,8 @@
         for lag, step in enumerate(steps):
             if 0 <= now - lag < len(DISTANCES):
                 step(now - lag, DISTANCES[now - lag])
+            if lag == 0 and now + 2 < len(DISTANCES):
+                send_y(now + 2, DISTANCES[now + 2])
     for k, e in enumerate(DISTANCES):
         if e:
             mirror(k, e)

time: 55 us -> 56.5 us (1.027)
  Pallas kernels: 52.4 us -> 54 us
    pallas_call x1, Pallas kernels: 52.4 us -> 54 us  [gram_tiles(): pl.pallas_call(functools.partial(gram_kernel, side), out_shape=jax.ShapeD...]
where the time goes in v6:
time: 56.5 us; the launch traced here: 56.3 us
  Pallas kernels  54 us (96%)
  local copies, waits for them, and re-layouts  2.31 us (4%)
    pallas_call x1, Pallas kernels, gram_tiles(): pl.pallas_call(functools.partial(gram_kernel, side), out_shape=jax.ShapeD...  54 us
    unnamed x1, local copies, waits for them, and re-layouts  2.31 us

profile of v6, /device:TPU:5, one launch (start us, length us, event | category | flops | bytes accessed | tf_op | source)
XLA Modules:
  0.0 56.3 jit_solution(5648196974691796845)
XLA Ops:
  0.0 54.0 %shard_map.55 = f32[256,1024]{1,0:T(8,128)} custom-call(f32[1,2048]{1,0:T(1,128)} %bitcast.3, s32[8,8]{1,0:T(8,128)} %mask_ref.1, s32[1,8]{1,0:T(1,128)} %bitcast.4, f32[1,4]{1,0:T(1,128)} %bitcast.5, bf16[1024,2048]{1,0:T(8,128)(2,1)} %s_ref.1), custom_call_target="tpu_custom_call" | custom-call | flops 5368709120 | bytes 4194304 | tf_op jit(solution)/shard_map/pallas_call | solution.py:255
  54.0 2.3 %copy.7 = f32[256,1024]{1,0:T(8,128)} copy(f32[256,1024]{1,0:T(8,128)} %shard_map.55) | data formatting | bytes 2097152
